TPU v7x, 32 devices: a whole 2x2x4 slice. The times are simulated.
32 devices in a mesh: ep: 16 (over z, y, core), tp: 2 (over x).
Axes of the slice: x: 2, y: 2, z: 4, core: 2. Of those that a mesh axis runs over, the one named last changes fastest.
Arguments:
- tokens_in: bfloat16 [16384, 1536], P('ep'), may hold values from -12 to 12
- lengths: int32 [16], P('ep'), may hold values from 1 to 1024, 8192 in all
- attn_gain: float32 [1536], replicated, may hold values from 0.1 to 1.9
- q_proj: float32 [1536, 1536], P('ep', 'tp'), may hold values from -2 to 2
- k_proj: float32 [1536, 512], P('ep', 'tp'), may hold values from -2 to 2
- value_projection: float32 [1536, 512], P('ep', 'tp'), may hold values from -0.15625 to 0.15625
- o_proj: float32 [1536, 1536], P('tp', 'ep'), may hold values from -2.5 to 2.5
- key_value_pages: bfloat16 [128, 16, 1024], P('ep', None, 'tp'), may hold values from -6 to 6
- page_table: int32 [16, 16, 2], P(None, 'ep'), may hold values from 0 to 7
- moe_gain: float32 [1536], replicated, may hold values from 0.1 to 1.9
- router: bfloat16 [1536, 16], replicated, may hold values from -5 to 5
- expert_ids: int32 [16384, 8], P(('ep', 'tp')), may hold values from 0 to 15, all different within a row; in each aligned block of 512 rows (0 to 511, 512 to 1023, ...) at most 384 rows name the same one
- gate_up_proj: float32 [16, 1536, 1024], P('ep', 'tp'), may hold values from -0.15625 to 0.15625
- down_proj: float32 [16, 512, 1536], P('ep', 'tp'), may hold values from -0.25 to 0.25
Outputs:
- layer_out: bfloat16 [16384, 1536], P(('ep', 'tp'))
Inputs may be any that keep to these rules, and one draw needn't show every extreme that they name: `expert_ids`: among the 512 token slots of each aligned block (one device's slots), no expert is named more than 384 times, a bound that some block reaches. `lengths`: some prompt is 1024 tokens long.
All inputs are finite; a program needn't handle non-finite values. No bound on the sum of `lengths` on one device may be relied on, other than what follows from the above.
Results may differ from a plain program's by a relative error of at most 0.018.
Values may be sent and summed in bfloat16 or wider, within the bound.
A program may use at most 192 MiB of HBM per device.

v0:
```python
import math

import jax
import jax.numpy as jnp
from jax import lax
from jax.sharding import PartitionSpec as P

QUERY_HEADS = 24
KEY_VALUE_HEADS = 8
HEAD_WIDTH = 64
FF = 512


epsilon = 1e-05


def rms_scale(values, norm_gain):
    mean_square = jnp.mean(values * values, axis=-1, keepdims=True)
    return values * lax.rsqrt(mean_square + epsilon) * norm_gain


def apply_rotary(vectors, token_positions):
    half_width = vectors.shape[-1] // 2
    frequency = jnp.exp(
        jnp.arange(half_width, dtype=jnp.float32) * (-2.0 * math.log(10000.0) / vectors.shape[-1])
    )
    angles = token_positions.astype(jnp.float32)[:, None] * frequency[None, :]
    cosine = jnp.cos(angles)[:, None, :]
    sine_table = jnp.sin(angles)[:, None, :]
    first_half = vectors[..., :half_width]
    second_half = vectors[..., half_width:]
    return jnp.concatenate(
        [
            first_half * cosine - second_half * sine_table,
            second_half * cosine + first_half * sine_table,
        ],
        axis=-1,
    )


def on_device(
    tokens_in,
    lengths,
    attn_gain,
    q_proj,
    k_proj,
    value_projection,
    o_proj,
    key_value_pages,
    page_table,
    moe_gain,
    router,
    expert_ids,
    gate_up_proj,
    down_proj,
):
    seq_len, model_width = tokens_in.shape
    ep_count = lax.axis_size("ep")
    tp_index = lax.axis_index("tp")
    heads_per_group = QUERY_HEADS // KEY_VALUE_HEADS
    kv_local = key_value_pages.shape[2] // (2 * HEAD_WIDTH)
    query_local = q_proj.shape[1] // HEAD_WIDTH
    query_weight, key_matrix, value_matrix, output_weight = (
        lax.all_gather(q_proj.astype(jnp.bfloat16), "ep", axis=0, tiled=True),
        lax.all_gather(k_proj.astype(jnp.bfloat16), "ep", axis=0, tiled=True),
        lax.all_gather(value_projection.astype(jnp.bfloat16), "ep", axis=0, tiled=True),
        lax.all_gather(o_proj.astype(jnp.bfloat16), "ep", axis=1, tiled=True),
    )
    chosen_pages = key_value_pages[page_table[:, 0, :]]
    arrived = lax.all_to_all(chosen_pages, "ep", split_axis=0, concat_axis=0, tiled=True)
    prefix_length = arrived.shape[0] * arrived.shape[1] * arrived.shape[2]
    prefix = arrived.reshape(prefix_length, kv_local, 2, HEAD_WIDTH)
    normalized_input = rms_scale(tokens_in.astype(jnp.float32), attn_gain).astype(jnp.bfloat16)
    token_positions = prefix_length + jnp.arange(seq_len)
    query_rows = apply_rotary(
        jnp.dot(normalized_input, query_weight, preferred_element_type=jnp.float32).reshape(
            seq_len, query_local, HEAD_WIDTH
        ),
        token_positions,
    ).astype(jnp.bfloat16)
    fresh_keys = apply_rotary(
        jnp.dot(normalized_input, key_matrix, preferred_element_type=jnp.float32).reshape(
            seq_len, kv_local, HEAD_WIDTH
        ),
        token_positions,
    ).astype(jnp.bfloat16)
    fresh_values = (
        jnp.dot(normalized_input, value_matrix, preferred_element_type=jnp.float32)
        .reshape(seq_len, kv_local, HEAD_WIDTH)
        .astype(jnp.bfloat16)
    )
    length_here = lengths[0]
    own = jnp.arange(prefix_length + seq_len)[None, :] - prefix_length
    block_rows = min(512, seq_len)
    head_outputs = []
    for kv_index in range(kv_local):
        all_keys = jnp.concatenate([prefix[:, kv_index, 0], fresh_keys[:, kv_index]], 0)
        all_values = jnp.concatenate([prefix[:, kv_index, 1], fresh_values[:, kv_index]], 0)
        grouped_queries = query_rows[
            :, kv_index * heads_per_group : (kv_index + 1) * heads_per_group
        ].transpose(1, 0, 2)
        blocks = []
        for block_start in range(0, seq_len, block_rows):
            query_block = grouped_queries[:, block_start : block_start + block_rows]
            scores = jnp.einsum(
                "gqd,kd->gqk", query_block, all_keys, preferred_element_type=jnp.float32
            ) * HEAD_WIDTH ** (-0.5)
            query_pos = block_start + jnp.arange(block_rows)
            allowed = (own < 0) | (own <= query_pos[:, None]) & (own < length_here)
            scores = jnp.where(allowed[None], scores, -1e30)
            top_score = jnp.max(scores, axis=-1, keepdims=True)
            weights = jnp.exp(scores - top_score)
            probs = (weights / jnp.sum(weights, axis=-1, keepdims=True)).astype(jnp.bfloat16)
            blocks.append(
                jnp.einsum(
                    "gqk,kd->gqd", probs, all_values, preferred_element_type=jnp.float32
                ).astype(jnp.bfloat16)
            )
        head_outputs.append(jnp.concatenate(blocks, axis=1))
    attended = (
        jnp.concatenate(head_outputs, axis=0)
        .transpose(1, 0, 2)
        .reshape(seq_len, query_local * HEAD_WIDTH)
    )
    partial_out = jnp.dot(attended, output_weight, preferred_element_type=jnp.float32)
    attn_sum = lax.psum_scatter(
        partial_out.astype(jnp.bfloat16), "tp", scatter_dimension=0, tiled=True
    ).astype(jnp.float32)
    row_count = attn_sum.shape[0]
    own_rows = lax.dynamic_slice_in_dim(tokens_in, tp_index * row_count, row_count, 0)
    hidden = own_rows.astype(jnp.float32) + attn_sum
    moe_in = rms_scale(hidden, moe_gain).astype(jnp.bfloat16)
    expert_count = router.shape[1]
    choose_count = expert_ids.shape[1]
    capacity = max(2, 3 * row_count * choose_count // (2 * expert_count))
    logits = jnp.dot(moe_in, router, preferred_element_type=jnp.float32)
    expert_range = jnp.arange(expert_count)
    matches = expert_ids[:, :, None] == expert_range[None, None, :]
    picked = jnp.sum(jnp.where(matches, logits[:, None, :], 0.0), axis=-1)
    top_logit = jnp.max(picked, axis=-1, keepdims=True)
    raised = jnp.exp(picked - top_logit)
    gates = raised / jnp.sum(raised, axis=-1, keepdims=True)
    flat_ids = expert_ids.reshape(-1)
    one_hot = (flat_ids[:, None] == expert_range[None, :]).astype(jnp.int32)
    earlier = jnp.cumsum(one_hot, axis=0) - one_hot
    slot_rank = jnp.sum(earlier * one_hot, axis=1)
    destination = flat_ids * capacity + slot_rank
    send_rows = (
        jnp.zeros((expert_count * capacity, model_width), jnp.bfloat16)
        .at[destination]
        .set(jnp.repeat(moe_in, choose_count, axis=0))
    )
    received = lax.all_to_all(
        send_rows.reshape(ep_count, -1, model_width), "ep", split_axis=0, concat_axis=0, tiled=True
    )
    exp_local = gate_up_proj.shape[0]
    batch_rows = ep_count * capacity
    batch = (
        received.reshape(ep_count, exp_local, capacity, model_width)
        .transpose(1, 0, 2, 3)
        .reshape(exp_local, batch_rows, model_width)
    )
    gate_up_local = gate_up_proj.astype(jnp.bfloat16)
    down_local = down_proj.astype(jnp.bfloat16)
    gate_up_full, down_full = (
        lax.all_gather(gate_up_local, "tp", axis=1, tiled=True),
        lax.all_gather(down_local, "tp", axis=1, tiled=True),
    )
    gate_up = jnp.einsum("erd,edf->erf", batch, gate_up_full, preferred_element_type=jnp.float32)
    activated = (jax.nn.silu(gate_up[..., :FF]) * gate_up[..., FF:]).astype(jnp.bfloat16)
    expert_out = jnp.einsum(
        "erf,efd->erd", activated, down_full, preferred_element_type=jnp.float32
    ).astype(jnp.bfloat16)
    outgoing = (
        expert_out.reshape(exp_local, ep_count, capacity, model_width)
        .transpose(1, 0, 2, 3)
        .reshape(ep_count, exp_local * capacity, model_width)
    )
    returned = lax.all_to_all(outgoing, "ep", split_axis=0, concat_axis=0, tiled=True).reshape(
        expert_count * capacity, model_width
    )
    picked_rows = (
        returned[destination].reshape(row_count, choose_count, model_width).astype(jnp.float32)
    )
    mixed = jnp.sum(picked_rows * gates[:, :, None], axis=1)
    valid = tp_index * row_count + jnp.arange(row_count) < length_here
    return jnp.where(valid[:, None], hidden + mixed, 0.0).astype(jnp.bfloat16)


def solution(mesh):
    in_specs = (
        P("ep", None),
        P("ep"),
        P(),
        P("ep", "tp"),
        P("ep", "tp"),
        P("ep", "tp"),
        P("tp", "ep"),
        P("ep", None, "tp"),
        P(None, "ep", None),
        P(),
        P(),
        P(("ep", "tp"), None),
        P("ep", "tp", None),
        P("ep", "tp", None),
    )
    out_specs = P(("ep", "tp"), None)
    return jax.shard_map(
        on_device, mesh=mesh, in_specs=in_specs, out_specs=out_specs, check_vma=False
    )
```

profile of v0, /device:TPU:13, one launch (start us, length us, event | category | flops | bytes accessed | tf_op | source)
XLA Modules:
  0.0 1328.2 jit_solution(12436188263559895529)
XLA Ops:
  10.6 6.6 all-to-all-start
  22.5 27.2 %all_gather.19 = bf16[1536,256]{1,0:T(8,128)(2,1)S(1)} all-gather(bf16[96,256]{1,0:T(8,128)(2,1)S(1)} %convert_element_type.142), channel_id=1, replica_groups=mesh['ep'=16,'tp'=2] {'ep'}, dimensions={0}, use_global_device_ids=true | all-gather | bytes 835584 | tf_op jit(solution)/shard_map/all_gather | solution.py:65
  51.3 18.4 %all_gather.20 = bf16[1536,256]{1,0:T(8,128)(2,1)S(1)} all-gather(bf16[96,256]{1,0:T(8,128)(2,1)S(1)} %convert_element_type.144), channel_id=1, replica_groups=mesh['ep'=16,'tp'=2] {'ep'}, dimensions={0}, use_global_device_ids=true | all-gather | bytes 835584 | tf_op jit(solution)/shard_map/all_gather | solution.py:66
  121.4 5.1 fusion.96
  126.5 5.1 fusion.88
  131.6 5.1 fusion.86
  136.6 5.4 fusion.84
  143.5 15.4 %fusion.151 = (f32[3,512]{1,0:T(4,128)}, f32[3,512,1536]{2,1,0:T(8,128)}) fusion(f32[3,512,1536]{2,1,0:T(8,128)} %fusion.88, pred[512,1536]{1,0:T(8,128)(4,1)} %get-tuple-element.29), kind=kOutput, calls=%fused_computation.241 | output fusion | flops 14157311 | bytes 19666944 | tf_op jit(solution)/shard_map/sub | solution.py:112
  158.9 15.1 %fusion.153 = (f32[3,512]{1,0:T(4,128)}, f32[3,512,1536]{2,1,0:T(8,128)}) fusion(f32[3,512,1536]{2,1,0:T(8,128)} %fusion.92, pred[512,1536]{1,0:T(8,128)(4,1)} %get-tuple-element.29), kind=kOutput, calls=%fused_computation.243 | output fusion | flops 14157311 | bytes 19666944 | tf_op jit(solution)/shard_map/sub | solution.py:112
  174.0 14.8 %fusion.152 = (f32[3,512]{1,0:T(4,128)S(1)}, f32[3,512,1536]{2,1,0:T(8,128)}) fusion(f32[3,512,1536]{2,1,0:T(8,128)} %fusion.90, pred[512,1536]{1,0:T(8,128)(4,1)} %get-tuple-element.30), kind=kOutput, calls=%fused_computation.242 | output fusion | flops 14157311 | bytes 19666944 | tf_op jit(solution)/shard_map/sub | solution.py:112
  188.8 15.2 %fusion.154 = (f32[3,512]{1,0:T(4,128)}, f32[3,512,1536]{2,1,0:T(8,128)}) fusion(f32[3,512,1536]{2,1,0:T(8,128)} %fusion.94, pred[512,1536]{1,0:T(8,128)(4,1)} %get-tuple-element.30), kind=kOutput, calls=%fused_computation.244 | output fusion | flops 14157311 | bytes 19666944 | tf_op jit(solution)/shard_map/sub | solution.py:112
  204.0 15.7 %fusion.155 = (f32[3,512]{1,0:T(4,128)}, f32[3,512,1536]{2,1,0:T(8,128)}) fusion(f32[3,512,1536]{2,1,0:T(8,128)} %fusion.96, pred[512,1536]{1,0:T(8,128)(4,1)} %get-tuple-element.29), kind=kOutput, calls=%fused_computation.245 | output fusion | flops 14157311 | bytes 19666944 | tf_op jit(solution)/shard_map/sub | solution.py:112
  219.8 15.8 %fusion.150 = (f32[3,512]{1,0:T(4,128)}, f32[3,512,1536]{2,1,0:T(8,128)}) fusion(f32[3,512,1536]{2,1,0:T(8,128)} %fusion.86, pred[512,1536]{1,0:T(8,128)(4,1)} %get-tuple-element.30), kind=kOutput, calls=%fused_computation.240 | output fusion | flops 14157311 | bytes 19666944 | tf_op jit(solution)/shard_map/sub | solution.py:112
  235.6 15.2 %fusion.149 = (f32[3,512]{1,0:T(4,128)}, f32[3,512,1536]{2,1,0:T(8,128)}) fusion(f32[3,512,1536]{2,1,0:T(8,128)} %fusion.84, pred[512,1536]{1,0:T(8,128)(4,1)} %get-tuple-element.29), kind=kOutput, calls=%fused_computation.239 | output fusion | flops 14157311 | bytes 19666944 | tf_op jit(solution)/shard_map/sub | solution.py:112
  250.8 5.4 fusion.67
  256.3 6.1 fusion.68
  270.0 10.0 fusion.148
  280.0 5.5 fusion.65
  285.5 5.4 fusion.64
  294.2 6.6 convolution_convert_fusion.1
  302.0 8.3 reduce-window.6
  313.3 33.3 %reduce-scatter.2.cloned.1.call-done = bf16[512,1536]{1,0:T(8,128)(2,1)} async-done(((bf16[1024,1536]{1,0:T(8,128)(2,1)}), bf16[512,1536]{1,0:T(8,128)(2,1)}) %reduce-scatter.2.cloned.1.call-update) | async-done | bytes 1572880 | tf_op jit(solution)/shard_map/reduce_scatter | solution.py:126
  351.7 29.9 %scatter_custom_fusion = bf16[6144,1536]{1,0:T(8,128)(2,1)} fusion(s32[4096]{0:T(1024)S(1)} %bitcast.154, bf16[]{:T(256)} %constant.12.clone.1, bf16[512,1536]{1,0:T(8,128)(2,1)} %multiply_convert_fusion), kind=kCustom, calls=%fused_computation.17 | custom fusion | bytes 20447234 | tf_op jit(solution)/shard_map/scatter | solution.py:151
  381.6 6.4 all-to-all-start.1
  393.8 42.3 %all-gather.9.cloned.1.call-done = bf16[1,1536,1024]{2,1,0:T(8,128)(2,1)} async-done(((bf16[1,768,1024]{2,1,0:T(8,128)(2,1)}), bf16[1,1536,1024]{2,1,0:T(8,128)(2,1)}) %all-gather.9.cloned.1.call-update) | async-done | bytes 3145744 | tf_op jit(solution)/shard_map/all_gather | solution.py:166
  436.1 358.9 %all-to-all-done.1 = bf16[16,384,1536]{2,1,0:T(8,128)(2,1)} async-done(((bf16[16,384,1536]{2,1,0:T(8,128)(2,1)}), bf16[16,384,1536]{2,1,0:T(8,128)(2,1)}, u32[]{:S(2)}, u32[]{:S(2)}) %all-to-all-start.1) | async-done | bytes 18874400 | tf_op jit(solution)/shard_map/all_to_all | solution.py:153
  795.0 26.5 %convolution_bitcast_fusion = f32[1,6144,1024]{2,1,0:T(8,128)} fusion(bf16[6144,1536]{1,0:T(8,128)(2,1)} %bitcast.41, bf16[1,1536,1024]{2,1,0:T(8,128)(2,1)} %all-gather.9.cloned.1.call-done), kind=kOutput, calls=%fused_computation.14 | convolution fusion | flops 19327352832 | bytes 47185920 | tf_op jit(solution)/shard_map/erd,edf->erf/dot_general | solution.py:169
  821.5 21.7 %convolution_convert_fusion = bf16[6144,1536]{1,0:T(8,128)(2,1)} fusion(f32[1,6144,1024]{2,1,0:T(8,128)} %convolution_bitcast_fusion, bf16[1,512,1536]{2,1,0:T(8,128)(2,1)} %all-gather.11.cloned.1.call-done), kind=kOutput, calls=%fused_computation.13 | convolution fusion | flops 9691987968 | bytes 45613056 | tf_op jit(solution)/shard_map/erf,efd->erd/dot_general | solution.py:171
  843.2 5.6 all-to-all-start.2
  851.6 404.1 %all-to-all-done.2 = bf16[16,384,1536]{2,1,0:T(8,128)(2,1)} async-done(((bf16[16,384,1536]{2,1,0:T(8,128)(2,1)}), bf16[16,384,1536]{2,1,0:T(8,128)(2,1)}, u32[]{:S(2)}, u32[]{:S(2)}) %all-to-all-start.2) | async-done | bytes 18874400 | tf_op jit(solution)/shard_map/all_to_all | solution.py:179
  1255.6 34.1 %gather_fusion.1 = bf16[4096,1536]{1,0:T(8,128)(2,1)} fusion(bf16[6144,1536]{1,0:T(8,128)(2,1)} %bitcast.47, s32[4096]{0:T(1024)S(1)} %broadcast_clamp_fusion), kind=kCustom, calls=%fused_computation.1 | custom fusion | bytes 25182208 | tf_op jit(solution)/shard_map/gather | solution.py:183
  1289.8 29.6 %fusion.8 = f32[512,1536]{1,0:T(8,128)S(1)} fusion(bf16[4096,1536]{1,0:T(8,128)(2,1)} %gather_fusion.1, f32[512,8]{1,0:T(8,128)S(1)} %copy.45), kind=kLoop, calls=%fused_computation.12 | loop fusion | flops 18087936 | bytes 15745024 | tf_op jit(solution)/shard_map/reduce_sum | solution.py:185
  (189 shorter events, 93.1 us)
Async XLA Ops:
  6.5 66.3 %copy-start.2 = (bf16[1024,1536]{1,0:T(8,128)(2,1)S(1)}, bf16[1024,1536]{1,0:T(8,128)(2,1)}, u32[]{:S(2)}) copy-start(bf16[1024,1536]{1,0:T(8,128)(2,1)} %param.14) | copy-start | bytes 9437188
  6.5 66.4 %copy-start.31 = (f32[1536]{0:T(1024)S(1)}, f32[1536]{0:T(1024)}, u32[]{:S(2)}) copy-start(f32[1536]{0:T(1024)} %param.16) | copy-start | bytes 18436
  6.5 94.4 %all-gather.5.cloned.1.call-start = ((), (), s32[]{:S(2)}) async-start(), calls=%async_computation.4 | async-start | bytes 2506752 | tf_op jit(solution)/shard_map/all_gather | solution.py:64
  10.6 69.1 %all-to-all-start = ((bf16[16,2,16,512]{3,2,1,0:T(8,128)(2,1)}), bf16[16,2,16,512]{3,2,1,0:T(8,128)(2,1)}, u32[]{:S(2)}, u32[]{:S(2)}) async-start(bf16[16,2,16,512]{3,2,1,0:T(8,128)(2,1)} %bitcast.132), calls=%async_computation | async-start | bytes 1048576 | tf_op jit(solution)/shard_map/all_to_all | solution.py:70
  17.2 277.0 %all-gather.7.cloned.1.call-start = ((), (), s32[]{:S(2)}) async-start(), calls=%async_computation.5 | async-start | bytes 2506752 | tf_op jit(solution)/shard_map/all_gather | solution.py:67
  18.9 327.7 %reduce-scatter.2.cloned.1.call-start = ((), (), s32[]{:S(2)}) async-start(), calls=%async_computation.6 | async-start | bytes 4718592 | tf_op jit(solution)/shard_map/reduce_scatter | solution.py:126
  235.6 15.2 %copy-start.22 = (bf16[1024,64]{0,1:T(8,128)(2,1)S(1)}, bf16[1024,64]{0,1:T(8,128)(2,1)}, u32[]{:S(2)}) copy-start(bf16[1024,64]{0,1:T(8,128)(2,1)} %get-tuple-element.24) | copy-start | bytes 393220
  235.6 15.2 %copy-start.26 = (bf16[512,1,1,64]{0,3,2,1:T(8,128)(2,1)S(1)}, bf16[512,1,1,64]{0,3,2,1:T(8,128)(2,1)}, u32[]{:S(2)}) copy-start(bf16[512,1,1,64]{0,3,2,1:T(8,128)(2,1)} %copy.49) | copy-start | bytes 196612
  250.8 11.7 slice-start.6
  250.8 11.7 slice-start.7
  256.3 6.2 copy-start.21
  256.3 6.2 copy-start.25
  256.3 6.2 slice-start.8
  256.3 6.2 copy-start.36
  256.3 9.0 slice-start.3
  256.3 8.9 slice-start.4
  280.0 5.5 copy-start.19
  280.0 5.5 copy-start.24
  280.0 5.5 copy-start.33
  280.0 10.9 slice-start.9
  280.0 10.9 slice-start.10
  294.1 6.7 copy-start.18
  294.2 52.4 %copy-start.3 = (bf16[1024,1536]{1,0:T(8,128)(2,1)S(1)}, bf16[1024,1536]{1,0:T(8,128)(2,1)}, u32[]{:S(2)}) copy-start(bf16[1024,1536]{1,0:T(8,128)(2,1)} %param.14) | copy-start | bytes 9437188
  300.8 47.8 %copy-start.29 = (f32[1536]{0:T(1024)S(1)}, f32[1536]{0:T(1024)}, u32[]{:S(2)}) copy-start(f32[1536]{0:T(1024)} %param.23) | copy-start | bytes 18436
  381.6 413.4 %all-to-all-start.1 = ((bf16[16,384,1536]{2,1,0:T(8,128)(2,1)}), bf16[16,384,1536]{2,1,0:T(8,128)(2,1)}, u32[]{:S(2)}, u32[]{:S(2)}) async-start(bf16[16,384,1536]{2,1,0:T(8,128)(2,1)} %bitcast.129), calls=%async_computation.2 | async-start | bytes 37748736 | tf_op jit(solution)/shard_map/all_to_all | solution.py:153
  388.0 48.1 %all-gather.9.cloned.1.call-start = ((), (), s32[]{:S(2)}) async-start(), calls=%async_computation.7 | async-start | bytes 4718592 | tf_op jit(solution)/shard_map/all_gather | solution.py:166
  391.3 430.2 %all-gather.11.cloned.1.call-start = ((), (), s32[]{:S(2)}) async-start(), calls=%async_computation.8 | async-start | bytes 2359296 | tf_op jit(solution)/shard_map/all_gather | solution.py:167
  843.2 6.2 copy-start.28
  843.2 412.4 %all-to-all-start.2 = ((bf16[16,384,1536]{2,1,0:T(8,128)(2,1)}), bf16[16,384,1536]{2,1,0:T(8,128)(2,1)}, u32[]{:S(2)}, u32[]{:S(2)}) async-start(bf16[16,384,1536]{2,1,0:T(8,128)(2,1)} %bitcast.130), calls=%async_computation.3 | async-start | bytes 37748736 | tf_op jit(solution)/shard_map/all_to_all | solution.py:179
  1255.6 65.5 %copy-start.1 = (bf16[8,16,512]{2,1,0:T(8,128)(2,1)S(1)}, bf16[8,16,512]{2,1,0:T(8,128)(2,1)}, u32[]{:S(2)}) copy-start(bf16[8,16,512]{2,1,0:T(8,128)(2,1)} %param.21) | copy-start | bytes 393220
  1289.8 29.6 %copy-start.4 = (bf16[512,1536]{1,0:T(8,128)(2,1)S(1)}, bf16[512,1536]{1,0:T(8,128)(2,1)}, u32[]{:S(2)}) copy-start(bf16[512,1536]{1,0:T(8,128)(2,1)} %reduce-scatter.2.cloned.1.call-done) | copy-start | bytes 4718596
  1289.8 29.6 %copy-start.30 = (pred[512]{0:T(512)(128)(4,1)S(1)}, pred[512]{0:T(512)(128)(4,1)}, u32[]{:S(2)}) copy-start(pred[512]{0:T(512)(128)(4,1)} %add_compare_fusion) | copy-start | bytes 1540
  (26 other events, 92.9 us)
Sparse Core Ops, SparseCore 0:
  9.6 48.1 all-gather.4
  60.1 41.4 all-gather.6
  300.9 45.6 reduce-scatter.1
  391.5 44.5 all-gather.8
  437.5 27.2 all-gather.10
where the time goes:
time: 1340 us; the launch traced here: 1330 us
  waiting for transfers between devices  839 us (63%)
  other arithmetic  185 us (14%)
  matrix products  134 us (10%)
  local copies, waits for them, and re-layouts  91.3 us (7%)
  blocking collectives  45.7 us (3%)
  starting transfers between devices  18.7 us (1%)
  between operations  15.1 us (1%)
    all_to_all x1, waiting for transfers between devices, on_device(): lax.all_to_all(outgoing, 'ep', split_axis=0, concat_axis=0, tiled=True)  404 us
    all_to_all x1, waiting for transfers between devices, on_device(): lax.all_to_all(send_rows.reshape(ep_count, -1, model_width), 'ep', split_...  359 us
    sub x8, other arithmetic, on_device(): weights = jnp.exp(scores - top_score)  117 us
    all_gather x1, waiting for transfers between devices, on_device(): lax.all_gather(gate_up_local, 'tp', axis=1, tiled=True)  42.3 us
    dot_general x8, matrix products, on_device(): jnp.einsum('gqd,kd->gqk', query_block, all_keys, preferred_element_type=j...  37 us
    gather x1, local copies, waits for them, and re-layouts, on_device(): returned[destination].reshape(row_count, choose_count, model_width)  34.1 us
    reduce_scatter x1, waiting for transfers between devices, on_device(): lax.psum_scatter(partial_out.astype(jnp.bfloat16), 'tp', scatter_dimensio...  33.3 us
    dot_general x8, matrix products, on_device(): jnp.einsum('gqk,kd->gqd', probs, all_values, preferred_element_type=jnp.f...  31.3 us
  transfers between devices with their start and end apart: 8, of which 4 were waited for; matrix products, arithmetic and copies ran while one was open for 21% of the time, Pallas kernels for 0%

commit v1 on v0

v1 whole, which is shorter than its diff:
```python
import math

import jax
import jax.numpy as jnp
from jax import lax
from jax.sharding import PartitionSpec as P

QUERY_HEADS = 24
KEY_VALUE_HEADS = 8
HEAD_WIDTH = 64
FF = 512


epsilon = 1e-05


def rms_scale(values, norm_gain):
    mean_square = jnp.mean(values * values, axis=-1, keepdims=True)
    return values * lax.rsqrt(mean_square + epsilon) * norm_gain


def apply_rotary(vectors, token_positions):
    half_width = vectors.shape[-1] // 2
    frequency = jnp.exp(
        jnp.arange(half_width, dtype=jnp.float32) * (-2.0 * math.log(10000.0) / vectors.shape[-1])
    )
    angles = token_positions.astype(jnp.float32)[:, None] * frequency[None, :]
    cosine = jnp.cos(angles)[:, None, :]
    sine_table = jnp.sin(angles)[:, None, :]
    first_half = vectors[..., :half_width]
    second_half = vectors[..., half_width:]
    return jnp.concatenate(
        [
            first_half * cosine - second_half * sine_table,
            second_half * cosine + first_half * sine_table,
        ],
        axis=-1,
    )


def on_device(
    tokens_in,
    lengths,
    attn_gain,
    q_proj,
    k_proj,
    value_projection,
    o_proj,
    key_value_pages,
    page_table,
    moe_gain,
    router,
    expert_ids,
    gate_up_proj,
    down_proj,
):
    seq_len, model_width = tokens_in.shape
    tp_index = lax.axis_index("tp")
    heads_per_group = QUERY_HEADS // KEY_VALUE_HEADS
    kv_local = key_value_pages.shape[2] // (2 * HEAD_WIDTH)
    query_local = q_proj.shape[1] // HEAD_WIDTH
    query_width = q_proj.shape[1]
    kv_width = k_proj.shape[1]
    qkv_weight = lax.all_gather(
        jnp.concatenate([q_proj, k_proj, value_projection], axis=1).astype(jnp.bfloat16),
        "ep",
        axis=0,
        tiled=True,
    )
    output_weight = lax.all_gather(o_proj.T.astype(jnp.bfloat16), "ep", axis=0, tiled=True)
    gate_up_full, down_full = (
        lax.all_gather(gate_up_proj.astype(jnp.bfloat16), "tp", axis=1, tiled=True),
        lax.all_gather(down_proj.astype(jnp.bfloat16), "tp", axis=1, tiled=True),
    )
    chosen_pages = key_value_pages[page_table[:, 0, :]]
    arrived = lax.all_to_all(chosen_pages, "ep", split_axis=0, concat_axis=0, tiled=True)
    prefix_length = arrived.shape[0] * arrived.shape[1] * arrived.shape[2]
    prefix = arrived.reshape(prefix_length, kv_local, 2, HEAD_WIDTH)
    normalized_input = rms_scale(tokens_in.astype(jnp.float32), attn_gain).astype(jnp.bfloat16)
    token_positions = prefix_length + jnp.arange(seq_len)
    qkv = jnp.dot(normalized_input, qkv_weight, preferred_element_type=jnp.float32)
    rotated = apply_rotary(
        qkv[:, : query_width + kv_width].reshape(seq_len, query_local + kv_local, HEAD_WIDTH),
        token_positions,
    ).astype(jnp.bfloat16)
    query_rows = rotated[:, :query_local]
    fresh_keys = rotated[:, query_local:]
    fresh_values = (
        qkv[:, query_width + kv_width :].reshape(seq_len, kv_local, HEAD_WIDTH).astype(jnp.bfloat16)
    )
    length_here = lengths[0]
    own = jnp.arange(prefix_length + seq_len)[None, :] - prefix_length
    block_rows = min(256, seq_len)
    head_outputs = []
    for kv_index in range(kv_local):
        all_keys = jnp.concatenate([prefix[:, kv_index, 0], fresh_keys[:, kv_index]], 0)
        all_values = jnp.concatenate([prefix[:, kv_index, 1], fresh_values[:, kv_index]], 0)
        grouped_queries = query_rows[
            :, kv_index * heads_per_group : (kv_index + 1) * heads_per_group
        ].transpose(1, 0, 2)
        blocks = []
        for block_start in range(0, seq_len, block_rows):
            query_block = grouped_queries[:, block_start : block_start + block_rows]
            key_count = prefix_length + block_start + block_rows
            scores = jnp.einsum(
                "gqd,kd->gqk", query_block, all_keys[:key_count], preferred_element_type=jnp.float32
            ) * HEAD_WIDTH ** (-0.5)
            query_pos = block_start + jnp.arange(block_rows)
            own_here = own[:, :key_count]
            allowed = (own_here < 0) | (own_here <= query_pos[:, None]) & (own_here < length_here)
            scores = jnp.where(allowed[None], scores, -1e30)
            top_score = jnp.max(scores, axis=-1, keepdims=True)
            weights = jnp.exp(scores - top_score)
            total = jnp.sum(weights, axis=-1, keepdims=True)
            mixed_values = jnp.einsum(
                "gqk,kd->gqd",
                weights.astype(jnp.bfloat16),
                all_values[:key_count],
                preferred_element_type=jnp.float32,
            )
            blocks.append((mixed_values / total).astype(jnp.bfloat16))
        head_outputs.append(jnp.concatenate(blocks, axis=1))
    attended = (
        jnp.concatenate(head_outputs, axis=0)
        .transpose(1, 0, 2)
        .reshape(seq_len, query_local * HEAD_WIDTH)
    )
    partial_out = lax.dot_general(
        attended, output_weight, (((1,), (1,)), ((), ())), preferred_element_type=jnp.float32
    )
    attn_sum = lax.psum_scatter(
        partial_out.astype(jnp.bfloat16), "tp", scatter_dimension=0, tiled=True
    ).astype(jnp.float32)
    row_count = attn_sum.shape[0]
    own_rows = lax.dynamic_slice_in_dim(tokens_in, tp_index * row_count, row_count, 0)
    hidden = own_rows.astype(jnp.float32) + attn_sum
    moe_in = rms_scale(hidden, moe_gain).astype(jnp.bfloat16)
    expert_count = router.shape[1]
    logits = jnp.dot(moe_in, router, preferred_element_type=jnp.float32)
    expert_range = jnp.arange(expert_count)
    matches = expert_ids[:, :, None] == expert_range[None, None, :]
    picked = jnp.sum(jnp.where(matches, logits[:, None, :], 0.0), axis=-1)
    top_logit = jnp.max(picked, axis=-1, keepdims=True)
    raised = jnp.exp(picked - top_logit)
    gates = raised / jnp.sum(raised, axis=-1, keepdims=True)
    gate_table = jnp.sum(jnp.where(matches, gates[:, :, None], 0.0), axis=1).T
    exp_local = gate_up_proj.shape[0]
    first_expert = lax.axis_index("ep") * exp_local
    chunk_count = 2
    chunk_rows = row_count // chunk_count
    gathered = [
        lax.all_gather(moe_in[c * chunk_rows : (c + 1) * chunk_rows], "ep", axis=0, tiled=True)
        for c in range(chunk_count)
    ]
    all_gates = lax.all_gather(gate_table, "ep", axis=0)
    own_gates = lax.dynamic_slice_in_dim(all_gates, first_expert, exp_local, 1)
    mixed_parts = []
    for c in range(chunk_count):
        rows = gathered[c]
        chunk_gates = own_gates[:, :, c * chunk_rows : (c + 1) * chunk_rows]
        weighted = 0.0
        for e in range(exp_local):
            gate_up = jnp.dot(rows, gate_up_full[e], preferred_element_type=jnp.float32)
            activated = (jax.nn.silu(gate_up[:, :FF]) * gate_up[:, FF:]).astype(jnp.bfloat16)
            expert_out = jnp.dot(activated, down_full[e], preferred_element_type=jnp.float32)
            weighted = weighted + expert_out * chunk_gates[:, e].reshape(-1)[:, None]
        mixed_parts.append(
            lax.psum_scatter(
                weighted.astype(jnp.bfloat16), "ep", scatter_dimension=0, tiled=True
            ).astype(jnp.float32)
        )
    mixed = jnp.concatenate(mixed_parts, axis=0)
    valid = tp_index * row_count + jnp.arange(row_count) < length_here
    return jnp.where(valid[:, None], hidden + mixed, 0.0).astype(jnp.bfloat16)


def solution(mesh):
    in_specs = (
        P("ep", None),
        P("ep"),
        P(),
        P("ep", "tp"),
        P("ep", "tp"),
        P("ep", "tp"),
        P("tp", "ep"),
        P("ep", None, "tp"),
        P(None, "ep", None),
        P(),
        P(),
        P(("ep", "tp"), None),
        P("ep", "tp", None),
        P("ep", "tp", None),
    )
    out_specs = P(("ep", "tp"), None)
    return jax.shard_map(
        on_device, mesh=mesh, in_specs=in_specs, out_specs=out_specs, check_vma=False
    )
```

time: 1340 us -> 798 us (0.60)
  waiting for transfers between devices: 839 us -> 519 us
  other arithmetic: 185 us -> 40.8 us
  local copies, waits for them, and re-layouts: 91.3 us -> 45.5 us
  blocking collectives: 45.7 us -> 16.9 us
  matrix products: 134 us -> 149 us
    all_to_all x2 -> x0, waiting for transfers between devices: 763 us -> none  [the longest x1 404 us: on_device(): lax.all_to_all(outgoing, 'ep', split_axis=0, concat_axis=0, tiled=True)]
    reduce_scatter x0 -> x2, waiting for transfers between devices: none -> 242 us  [on_device(): lax.psum_scatter(weighted.astype(jnp.bfloat16), 'ep', scatter_dimension=0...]
    all_gather x4 -> x6, waiting for transfers between devices: 42.3 us -> 224 us  [the longest x2 189 us: on_device(): lax.all_gather(moe_in[c * chunk_rows:(c + 1) * chunk_rows], 'ep', axis=0,...]
    sub x8 -> x0, other arithmetic: 117 us -> none  [on_device(): weights = jnp.exp(scores - top_score)]
    gather x1 -> x0, local copies, waits for them, and re-layouts: 34.1 us -> none  [on_device(): returned[destination].reshape(row_count, choose_count, model_width)]
    scatter x1 -> x0, local copies, waits for them, and re-layouts: 29.9 us -> none  [on_device(): send_rows = jnp.zeros((expert_count * capacity, model_width), jnp.bfloat1...]
    all_gather x2 -> x1, blocking collectives: 45.7 us -> 16.9 us  [on_device(): all_gates = lax.all_gather(gate_table, 'ep', axis=0)]
    reduce_sum x2 -> x8, other arithmetic: 29.8 us -> 11 us  [the longest x7 10.9 us: on_device(): total = jnp.sum(weights, axis=-1, keepdims=True)]
  transfers between devices with their start and end apart: 8 -> 10, of which waited for: 4 -> 9; matrix products, arithmetic and copies ran while one was open for 21% -> 27% of each run, Pallas kernels for 0% -> 0%
where the time goes in v1:
time: 798 us; the launch traced here: 794 us
  waiting for transfers between devices  519 us (65%)
  matrix products  149 us (19%)
  local copies, waits for them, and re-layouts  45.5 us (6%)
  other arithmetic  40.8 us (5%)
  blocking collectives  16.9 us (2%)
  between operations  14.7 us (2%)
    reduce_scatter x2, waiting for transfers between devices, on_device(): lax.psum_scatter(weighted.astype(jnp.bfloat16), 'ep', scatter_dimension=0...  242 us
    all_gather x2, waiting for transfers between devices, on_device(): lax.all_gather(moe_in[c * chunk_rows:(c + 1) * chunk_rows], 'ep', axis=0,...  189 us
    dot_general x16, matrix products, on_device(): jnp.einsum('gqd,kd->gqk', query_block, all_keys[:key_count], preferred_el...  51.4 us
    reduce_scatter x1, waiting for transfers between devices, on_device(): lax.psum_scatter(partial_out.astype(jnp.bfloat16), 'tp', scatter_dimensio...  39.1 us
    dot_general x2, matrix products, on_device(): gate_up = jnp.dot(rows, gate_up_full[e], preferred_element_type=jnp.float32)  38.9 us
    dot_general x2, matrix products, on_device(): jnp.dot(activated, down_full[e], preferred_element_type=jnp.float32)  28.4 us
    unnamed x98, local copies, waits for them, and re-layouts  21.2 us
    all_gather x1, waiting for transfers between devices, on_device(): lax.all_gather(gate_up_proj.astype(jnp.bfloat16), 'tp', axis=1, tiled=True)  18.5 us
  transfers between devices with their start and end apart: 10, of which 9 were waited for; matrix products, arithmetic and copies ran while one was open for 27% of the time, Pallas kernels for 0%

profile of v1, /device:TPU:13, one launch (start us, length us, event | category | flops | bytes accessed | tf_op | source)
XLA Modules:
  0.0 793.7 jit_solution(7377630483911989892)
XLA Ops:
  12.5 6.6 all-to-all-start
  27.6 13.1 %all-to-all-done = bf16[16,2,16,512]{3,2,1,0:T(8,128)(2,1)} async-done(((bf16[16,2,16,512]{3,2,1,0:T(8,128)(2,1)}), bf16[16,2,16,512]{3,2,1,0:T(8,128)(2,1)}, u32[]{:S(2)}, u32[]{:S(2)}) %all-to-all-start) | async-done | bytes 524320 | tf_op jit(solution)/shard_map/all_to_all | solution.py:76
  40.6 3.5 reshape.457
  44.1 4.0 fusion.407
  60.6 6.8 all-gather.8.cloned.1.call-done
  67.5 6.4 fusion.33
  78.9 5.7 copy.38
  84.6 2.9 subtract_convert_fusion
  91.3 2.9 fusion.224
  96.5 3.0 fusion.229
  105.5 2.9 fusion.408
  108.3 2.8 fusion.409
  111.1 2.8 fusion.411
  114.0 3.2 fusion.9
  126.3 14.8 %fusion.45 = (f32[3,256]{1,0:T(4,128)S(1)}, f32[3,256]{1,0:T(4,128)S(1)}, f32[3,256]{1,0:T(4,128)S(1)}, f32[3,256]{1,0:T(4,128)S(1)}, f32[3,256,1024]{2,1,0:T(8,128)S(1)}) fusion(f32[3,256,1024]{2,1,0:T(8,128)S(1)} %get-tuple-element.66, f32[3,256]{1,0:T(4,128)S(1)} %get-tuple-element.65, pred[256,1024]{1,0:T(8,128)(4,1)S(1)} %copy-done.15, ...), kind=kOutput, calls=%fused_computation.92 | convolution fusion | flops 111145984 | bytes 13156352 | tf_op jit(solution)/shard_map/gqd,kd->gqk/dot_general | solution.py:105
  165.0 4.2 fusion.17
  169.1 3.6 fusion.19
  179.5 6.5 convolution_convert_fusion
  186.1 3.3 convert_element_type.204
  189.4 39.1 %reduce-scatter.4.cloned.1.call-done = bf16[512,1536]{1,0:T(8,128)(2,1)} async-done(((bf16[1024,1536]{1,0:T(8,128)(2,1)}), bf16[512,1536]{1,0:T(8,128)(2,1)}) %reduce-scatter.4.cloned.1.call-update) | async-done | bytes 1572880 | tf_op jit(solution)/shard_map/reduce_scatter | solution.py:131
  239.4 16.9 %all-gather = f32[256,512]{1,0:T(8,128)S(1)} all-gather(f32[16,512]{1,0:T(8,128)S(1)} %bitcast.223), channel_id=2, replica_groups=mesh['ep'=16,'tp'=2] {'ep'}, dimensions={0}, use_global_device_ids=true | all-gather | bytes 557056 | tf_op jit(solution)/shard_map/all_gather | solution.py:155
  256.5 18.5 %all-gather.14.cloned.1.call-done = bf16[1,1536,1024]{2,1,0:T(8,128)(2,1)} async-done(((bf16[1,768,1024]{2,1,0:T(8,128)(2,1)}), bf16[1,1536,1024]{2,1,0:T(8,128)(2,1)}) %all-gather.14.cloned.1.call-update) | async-done | bytes 3145744 | tf_op jit(solution)/shard_map/all_gather | solution.py:72
  275.0 101.4 %all-gather.18.cloned.1.call-done = bf16[4096,1536]{1,0:T(8,128)(2,1)} async-done(((bf16[256,1536]{1,0:T(8,128)(2,1)}), bf16[4096,1536]{1,0:T(8,128)(2,1)}) %all-gather.18.cloned.1.call-update) | async-done | bytes 12582928 | tf_op jit(solution)/shard_map/all_gather | solution.py:152
  376.3 19.2 %fusion.35 = f32[4096,1024]{1,0:T(8,128)} fusion(bf16[4096,1536]{1,0:T(8,128)(2,1)} %all-gather.18.cloned.1.call-done, bf16[1,1536,1024]{2,1,0:T(8,128)(2,1)} %all-gather.14.cloned.1.call-done), kind=kOutput, calls=%fused_computation.70 | convolution fusion | flops 12884901888 | bytes 32505856 | tf_op jit(solution)/shard_map/dot_general | solution.py:163
  395.5 9.5 %all-gather.16.cloned.1.call-done = bf16[1,512,1536]{2,1,0:T(8,128)(2,1)} async-done(((bf16[1,256,1536]{2,1,0:T(8,128)(2,1)}), bf16[1,512,1536]{2,1,0:T(8,128)(2,1)}) %all-gather.16.cloned.1.call-update) | async-done | bytes 1572880 | tf_op jit(solution)/shard_map/all_gather | solution.py:73
  405.0 13.8 %multiply_convert_fusion = bf16[4096,1536]{1,0:T(8,128)(2,1)} fusion(f32[4096]{0:T(1024)S(1)} %bitcast.234, f32[4096,1024]{1,0:T(8,128)} %fusion.35, bf16[1,512,1536]{2,1,0:T(8,128)(2,1)} %all-gather.16.cloned.1.call-done), kind=kOutput, calls=%fused_computation.1 | convolution fusion | flops 6467616768 | bytes 30949376 | tf_op jit(solution)/shard_map/dot_general | solution.py:165
  419.1 87.5 %all-gather.12.cloned.1.call-done = bf16[4096,1536]{1,0:T(8,128)(2,1)} async-done(((bf16[256,1536]{1,0:T(8,128)(2,1)}), bf16[4096,1536]{1,0:T(8,128)(2,1)}) %all-gather.12.cloned.1.call-update) | async-done | bytes 12582928 | tf_op jit(solution)/shard_map/all_gather | solution.py:152
  506.6 19.7 %fusion.37 = f32[4096,1024]{1,0:T(8,128)} fusion(bf16[4096,1536]{1,0:T(8,128)(2,1)} %all-gather.12.cloned.1.call-done, bf16[1,1536,1024]{2,1,0:T(8,128)(2,1)} %all-gather.14.cloned.1.call-done), kind=kOutput, calls=%fused_computation.72 | convolution fusion | flops 12884901888 | bytes 32505856 | tf_op jit(solution)/shard_map/dot_general | solution.py:163
  526.3 14.7 %multiply_convert_fusion.1 = bf16[4096,1536]{1,0:T(8,128)(2,1)} fusion(f32[4096]{0:T(1024)S(1)} %bitcast.233, f32[4096,1024]{1,0:T(8,128)} %fusion.37, bf16[1,512,1536]{2,1,0:T(8,128)(2,1)S(1)} %copy-done.37), kind=kOutput, calls=%fused_computation.2 | convolution fusion | flops 6467616768 | bytes 30949376 | tf_op jit(solution)/shard_map/dot_general | solution.py:165
  541.0 103.9 %reduce-scatter.8.cloned.1.call-done = bf16[256,1536]{1,0:T(8,128)(2,1)} async-done(((bf16[4096,1536]{1,0:T(8,128)(2,1)}), bf16[256,1536]{1,0:T(8,128)(2,1)}) %reduce-scatter.8.cloned.1.call-update) | async-done | bytes 786448 | tf_op jit(solution)/shard_map/reduce_scatter | solution.py:168
  644.9 138.4 %reduce-scatter.6.cloned.1.call-done = bf16[256,1536]{1,0:T(8,128)(2,1)} async-done(((bf16[4096,1536]{1,0:T(8,128)(2,1)}), bf16[256,1536]{1,0:T(8,128)(2,1)}) %reduce-scatter.6.cloned.1.call-update) | async-done | bytes 786448 | tf_op jit(solution)/shard_map/reduce_scatter | solution.py:168
  783.2 3.7 select_convert_fusion
  (201 shorter events, 94.0 us)
Async XLA Ops:
  6.5 4.5 copy-start
  6.5 14.4 %copy-start.2 = (bf16[1024,1536]{1,0:T(8,128)(2,1)S(1)}, bf16[1024,1536]{1,0:T(8,128)(2,1)}, u32[]{:S(2)}) copy-start(bf16[1024,1536]{1,0:T(8,128)(2,1)} %param.14) | copy-start | bytes 9437188
  6.5 60.9 %all-gather.8.cloned.1.call-start = ((), (), s32[]{:S(2)}) async-start(), calls=%async_computation.4 | async-start | bytes 4177920 | tf_op jit(solution)/shard_map/all_gather | solution.py:64
  12.5 28.2 %all-to-all-start = ((bf16[16,2,16,512]{3,2,1,0:T(8,128)(2,1)}), bf16[16,2,16,512]{3,2,1,0:T(8,128)(2,1)}, u32[]{:S(2)}, u32[]{:S(2)}) async-start(bf16[16,2,16,512]{3,2,1,0:T(8,128)(2,1)} %bitcast.195), calls=%async_computation | async-start | bytes 1048576 | tf_op jit(solution)/shard_map/all_to_all | solution.py:76
  19.0 160.5 %all-gather.10.cloned.1.call-start = ((), (), s32[]{:S(2)}) async-start(), calls=%async_computation.5 | async-start | bytes 2506752 | tf_op jit(solution)/shard_map/all_gather | solution.py:70
  20.7 207.8 %reduce-scatter.4.cloned.1.call-start = ((), (), s32[]{:S(2)}) async-start(), calls=%async_computation.6 | async-start | bytes 4718592 | tf_op jit(solution)/shard_map/reduce_scatter | solution.py:131
  44.1 23.4 %copy-start.38 = (f32[1536]{0:T(1024)S(1)}, f32[1536]{0:T(1024)}, u32[]{:S(2)}) copy-start(f32[1536]{0:T(1024)} %param.16) | copy-start | bytes 18436
  78.9 5.7 copy-start.19
  87.5 3.8 copy-start.17
  88.2 25.7 %copy-start.29 = (bf16[1024,64]{0,1:T(8,128)(2,1)}, bf16[1024,64]{0,1:T(8,128)(2,1)S(1)}, u32[]{:S(2)}) copy-start(bf16[1024,64]{0,1:T(8,128)(2,1)S(1)} %get-tuple-element.39) | copy-start | bytes 393220
  89.1 24.8 %copy-start.21 = (bf16[3,1024,64]{1,2,0:T(8,128)(2,1)}, bf16[3,1024,64]{1,2,0:T(8,128)(2,1)S(1)}, u32[]{:S(2)}) copy-start(bf16[3,1024,64]{1,2,0:T(8,128)(2,1)S(1)} %get-tuple-element.35) | copy-start | bytes 1179652
  91.3 5.1 copy-start.16
  101.7 3.8 copy-start.22
  113.9 6.6 copy-start.15
  119.2 3.2 copy-start.5
  143.5 3.1 copy-start.10
  143.5 3.1 copy-start.11
  156.3 7.4 slice-start.4
  160.2 3.5 slice-start.5
  161.0 3.5 slice-start.2
  161.9 3.0 slice-start.3
  186.0 89.0 %all-gather.14.cloned.1.call-start = ((), (), s32[]{:S(2)}) async-start(), calls=%async_computation.8 | async-start | bytes 4718592 | tf_op jit(solution)/shard_map/all_gather | solution.py:72
  189.3 41.3 %copy-start.36 = (f32[1536]{0:T(1024)S(1)}, f32[1536]{0:T(1024)}, u32[]{:S(2)}) copy-start(f32[1536]{0:T(1024)} %param.23) | copy-start | bytes 18436
  189.4 187.0 %all-gather.18.cloned.1.call-start = ((), (), s32[]{:S(2)}) async-start(), calls=%async_computation.11 | async-start | bytes 13369344 | tf_op jit(solution)/shard_map/all_gather | solution.py:152
  233.7 3.5 copy-start.35
  233.7 5.6 copy-start.34
  233.7 171.3 %all-gather.16.cloned.1.call-start = ((), (), s32[]{:S(2)}) async-start(), calls=%async_computation.9 | async-start | bytes 2359296 | tf_op jit(solution)/shard_map/all_gather | solution.py:73
  236.1 270.4 %all-gather.12.cloned.1.call-start = ((), (), s32[]{:S(2)}) async-start(), calls=%async_computation.7 | async-start | bytes 13369344 | tf_op jit(solution)/shard_map/all_gather | solution.py:152
  236.9 408.0 %reduce-scatter.8.cloned.1.call-start = ((), (), s32[]{:S(2)}) async-start(), calls=%async_computation.12 | async-start | bytes 13369344 | tf_op jit(solution)/shard_map/reduce_scatter | solution.py:168
  418.8 364.4 %reduce-scatter.6.cloned.1.call-start = ((), (), s32[]{:S(2)}) async-start(), calls=%async_computation.10 | async-start | bytes 13369344 | tf_op jit(solution)/shard_map/reduce_scatter | solution.py:168
  506.6 19.7 %copy-start.37 = (bf16[1,512,1536]{2,1,0:T(8,128)(2,1)S(1)}, bf16[1,512,1536]{2,1,0:T(8,128)(2,1)}, u32[]{:S(2)}) copy-start(bf16[1,512,1536]{2,1,0:T(8,128)(2,1)} %all-gather.16.cloned.1.call-done) | copy-start | bytes 4718596
  541.0 245.9 %copy-start.1 = (bf16[8,16,512]{2,1,0:T(8,128)(2,1)S(1)}, bf16[8,16,512]{2,1,0:T(8,128)(2,1)}, u32[]{:S(2)}) copy-start(bf16[8,16,512]{2,1,0:T(8,128)(2,1)} %param.21) | copy-start | bytes 393220
  (23 other events, 47.1 us)
Sparse Core Ops, SparseCore 0:
  10.3 57.0 all-gather.7
  69.7 40.1 all-gather.9
  186.1 42.3 reduce-scatter.3
  230.0 44.9 all-gather.13
  277.4 98.9 all-gather.17
  377.8 27.1 all-gather.15
  407.6 98.9 all-gather.11
  511.1 133.6 reduce-scatter.7
  649.5 133.7 reduce-scatter.5
